TPU v7x, 32 devices: a whole 2x2x4 slice. The times are simulated.
32 devices in a mesh: lat: 2 (over x), lon: 16 (over z, y, core).
Axes of the slice: x: 2, y: 2, z: 4, core: 2. Of those that a mesh axis runs over, the one named last changes fastest.
Arguments:
- tracer: float32 [4, 512, 2048], P(None, 'lat', 'lon'), may hold values from -6 to 6
- wind_east: float32 [4, 512, 2048], P(None, 'lat', 'lon'), may hold values from -4 to 4
- wind_north: float32 [4, 512, 2048], P(None, 'lat', 'lon'), may hold values from -4 to 4
- kappa: float32 [4, 512, 2048], P(None, 'lat', 'lon'), may hold values from 0.25 to 4
- cutoff: int32 [128], replicated, may hold values from 64 to 511
- partner: int32 [2048], replicated, may hold values from 0 to 2047, as said below
Outputs:
- filtered: float32 [4, 512, 2048], P(None, 'lat', 'lon')
- balanced: float32 [4, 512, 2048], P(None, 'lat', 'lon')
Inputs may be any that keep to these rules, and one draw needn't show every extreme that they name: partner[j] = (j + 1024 + s_j) mod 2048 with each column's own shift s_j of 0 to 127; some column has s_j = 127.
All inputs are finite; a program needn't handle non-finite values.
Results may differ from a plain program's by a relative error of at most 0.00005.
Values sent between devices are 32-bit elements; how exact they have to be, the bound alone decides.
A program may use at most 64 MiB of HBM per device.

v0:
```python
import math
import jax
import jax.numpy as jnp
from jax import lax
from jax.sharding import PartitionSpec as P

KMAX = 512
SWEEPS = 4
COURANT = 0.4


def padded(cells, sides, width, closed):
    for axis, dim in sides:
        count = lax.axis_size(axis)
        ends = count if closed else count - 1
        head = lax.slice_in_dim(cells, 0, width, axis=dim)
        tail = lax.slice_in_dim(cells, cells.shape[dim] - width, cells.shape[dim], axis=dim)
        cells = jnp.concatenate(
            [
                lax.ppermute(tail, axis, [(i, (i + 1) % count) for i in range(ends)]),
                cells,
                lax.ppermute(head, axis, [((i + 1) % count, i) for i in range(ends)]),
            ],
            axis=dim,
        )
    return cells


def neighbours(field, partner):
    width = field.shape[2]
    lon_index = lax.axis_index("lon")
    lon_padded = padded(field, (("lon", 2),), 1, True)
    lat_padded = padded(field, (("lat", 1),), 1, False)
    edge_rows = jnp.stack([field[:, 0, :], field[:, -1, :]], axis=1)
    own_partner = lax.dynamic_slice_in_dim(partner, lon_index * width, width)
    whole_rows = lax.all_gather(edge_rows, "lon", axis=2, tiled=True)
    across = jnp.take(whole_rows, own_partner, axis=2)
    lat_index = lax.axis_index("lat")
    last_band = lax.axis_size("lat") - 1
    upper_row = jnp.where(lat_index == 0, across[:, 0, :], lat_padded[:, 0, :])
    lower_row = jnp.where(lat_index == last_band, across[:, 1, :], lat_padded[:, -1, :])
    upper = jnp.concatenate([upper_row[:, None, :], field[:, :-1, :]], axis=1)
    lower = jnp.concatenate([field[:, 1:, :], lower_row[:, None, :]], axis=1)
    western = lon_padded[:, :, :-2]
    eastern = lon_padded[:, :, 2:]
    return (western, eastern, upper, lower)


def tables(start, count, total, kmaximum):
    columns = start + jnp.arange(count, dtype=jnp.int32)
    waves = jnp.arange(kmaximum, dtype=jnp.int32)
    phase = columns[:, None] * waves[None, :] % total
    angle = phase.astype(jnp.float32) * (2.0 * math.pi / total)
    return (jnp.cos(angle), jnp.sin(angle))


def project(rows, start, total, kmaximum):
    cosine, sine = tables(start, rows.shape[1], total, kmaximum)
    cos_part = jnp.dot(
        rows, cosine, precision=lax.Precision.HIGHEST, preferred_element_type=jnp.float32
    )
    sin_part = jnp.dot(
        rows, sine, precision=lax.Precision.HIGHEST, preferred_element_type=jnp.float32
    )
    return (cos_part, sin_part)


def rebuild(cos_part, sin_part, limits, start, count, total):
    kmaximum = cos_part.shape[1]
    waves = jnp.arange(kmaximum, dtype=jnp.int32)
    weights = jnp.where(waves == 0, 1.0, 2.0).astype(jnp.float32) / total
    scaled = jnp.where(waves[None, :] <= limits[:, None], weights[None, :], 0.0)
    cosine, sine = tables(start, count, total, kmaximum)
    contract = (((1,), (1,)), ((), ()))
    first_term = lax.dot_general(
        cos_part * scaled,
        cosine,
        contract,
        precision=lax.Precision.HIGHEST,
        preferred_element_type=jnp.float32,
    )
    second_term = lax.dot_general(
        sin_part * scaled,
        sine,
        contract,
        precision=lax.Precision.HIGHEST,
        preferred_element_type=jnp.float32,
    )
    return first_term + second_term


def polar_filter(field, cutoff):
    levels, band_rows, width = field.shape
    pole_rows = cutoff.shape[0] // 2
    sectors = lax.axis_size("lon")
    total = width * sectors
    lon_index = lax.axis_index("lon")
    lat_index = lax.axis_index("lat")
    is_north = lat_index == 0
    is_south = lat_index == lax.axis_size("lat") - 1
    band = jnp.where(is_north, field[:, :pole_rows, :], field[:, band_rows - pole_rows :, :])
    band_limits = jnp.where(is_north, cutoff[:pole_rows], cutoff[pole_rows:])
    flat = band.reshape(levels * pole_rows, width)
    row_limits = jnp.tile(band_limits, levels)
    own_start = lon_index * width
    cos_add, sin_add = project(
        lax.all_gather(flat, "lon", axis=1, tiled=True), jnp.int32(0), total, KMAX
    )
    smooth = rebuild(cos_add, sin_add, row_limits, own_start, width, total)
    smooth = smooth.reshape(levels, pole_rows, width)
    top_rows = jnp.where(is_north, smooth, field[:, :pole_rows, :])
    bottom_rows = jnp.where(is_south, smooth, field[:, band_rows - pole_rows :, :])
    return jnp.concatenate(
        [top_rows, field[:, pole_rows : band_rows - pole_rows, :], bottom_rows], axis=1
    )


def per_device(tracer, wind_east, wind_north, kappa, cutoff, partner):
    western, eastern, upper, lower = neighbours(tracer, partner)
    advected = tracer - COURANT * 0.5 * (
        wind_east * (eastern - western) + wind_north * (lower - upper)
    )
    filtered = polar_filter(advected, cutoff)
    balanced = filtered
    for sweep_index in range(SWEEPS):
        western, eastern, upper, lower = neighbours(balanced, partner)
        balanced = (filtered + kappa * (western + eastern + upper + lower)) / (1.0 + 4.0 * kappa)
    return (filtered, balanced)


def solution(mesh):
    in_specs = (
        P(None, "lat", "lon"),
        P(None, "lat", "lon"),
        P(None, "lat", "lon"),
        P(None, "lat", "lon"),
        P(),
        P(),
    )
    out_specs = (P(None, "lat", "lon"), P(None, "lat", "lon"))
    return jax.shard_map(
        per_device, mesh=mesh, in_specs=in_specs, out_specs=out_specs, check_vma=False
    )
```

profile of v0, /device:TPU:3, one launch (start us, length us, event | category | flops | bytes accessed | tf_op | source)
XLA Modules:
  0.0 317.8 jit_solution(2903918422624642746)
XLA Ops:
  10.6 2.3 fusion.88
  13.6 2.3 collective-permute-start.1
  17.7 23.6 %all_gather.18 = f32[4,2,2048]{2,0,1:T(4,128)S(1)} all-gather(f32[4,2,128]{2,0,1:T(4,128)S(1)} %pad_maximum_fusion.15), channel_id=1, replica_groups=mesh['lat'=2,'lon'=16] {'lon'}, dimensions={2}, use_global_device_ids=true | all-gather | bytes 69632 | tf_op jit(solution)/shard_map/all_gather | solution.py:36
  44.1 2.3 fusion.46
  47.3 40.6 %all-gather.2.cloned.1.call-done = f32[256,2048]{1,0:T(8,128)} async-done(((f32[256,128]{1,0:T(8,128)}), f32[256,2048]{1,0:T(8,128)}) %all-gather.2.cloned.1.call-update) | async-done | bytes 2097168 | tf_op jit(solution)/shard_map/all_gather | solution.py:107
  87.8 21.2 %fusion.12 = f32[256,512]{1,0:T(8,128)S(1)} fusion(f32[256,2048]{1,0:T(8,128)} %all-gather.2.cloned.1.call-done, f32[512]{0:T(512)S(1)} %select_multiply_fusion, s32[256]{0:T(256)S(1)} %le.23), kind=kOutput, calls=%fused_computation.18 | convolution fusion | flops 3236298752 | bytes 2624512 | tf_op jit(solution)/shard_map/dot_general | solution.py:59
  109.1 1.6 fusion.52
  110.7 19.7 %fusion.15 = f32[256,512]{1,0:T(8,128)S(1)} fusion(f32[256,2048]{1,0:T(8,128)S(1)} %copy-done.5, f32[512]{0:T(512)S(1)} %select_multiply_fusion, s32[256]{0:T(256)S(1)} %le.23), kind=kOutput, calls=%fused_computation.19 | convolution fusion | flops 3236298752 | bytes 2624512 | tf_op jit(solution)/shard_map/dot_general | solution.py:62
  130.3 1.6 convolution_add_fusion
  135.6 4.0 %collective-permute-start.7 = (f32[4,1,128]{2,1,0:T(1,128)S(1)}, f32[4,1,128]{2,1,0:T(1,128)S(1)}, u32[]{:S(2)}, u32[]{:S(2)}) collective-permute-start(f32[4,1,128]{2,1,0:T(1,128)S(1)} %slice.259), channel_id=1, source_target_pairs={{16,0},{17,1},{18,2},{19,3},{20,4},{21,5},{22,6},{23,7},{24,8},{25... | collective-permute-start | bytes 6152 | tf_op jit(solution)/shard_map/ppermute | solution.py:22
  139.6 20.1 %all_gather.20 = f32[4,2,2048]{2,0,1:T(4,128)S(1)} all-gather(f32[4,2,128]{2,0,1:T(4,128)S(1)} %pad_maximum_fusion.16), channel_id=1, replica_groups=mesh['lat'=2,'lon'=16] {'lon'}, dimensions={2}, use_global_device_ids=true | all-gather | bytes 69632 | tf_op jit(solution)/shard_map/all_gather | solution.py:36
  162.2 11.5 %collective-permute-done.4 = f32[4,256,1]{2,1,0:T(8,128)S(1)} collective-permute-done((f32[4,256,1]{2,1,0:T(8,128)}, f32[4,256,1]{2,1,0:T(8,128)S(1)}, u32[]{:S(2)}, u32[]{:S(2)}) %collective-permute-start.4) | collective-permute-done | bytes 4128 | tf_op jit(solution)/shard_map/ppermute | solution.py:20
  173.7 2.4 collective-permute-done.5
  176.2 1.7 fusion.41
  180.3 4.0 %collective-permute-start.11 = (f32[4,1,128]{2,1,0:T(1,128)S(1)}, f32[4,1,128]{2,1,0:T(1,128)S(1)}, u32[]{:S(2)}, u32[]{:S(2)}) collective-permute-start(f32[4,1,128]{2,1,0:T(1,128)S(1)} %get-tuple-element.29), channel_id=1, source_target_pairs={{16,0},{17,1},{18,2},{19,3},{20,4},{21,5},{22,6},{23,7},{24,8},{25... | collective-permute-start | bytes 6152 | tf_op jit(solution)/shard_map/ppermute | solution.py:22
  184.3 18.0 %all_gather.21 = f32[4,2,2048]{2,0,1:T(4,128)S(1)} all-gather(f32[4,2,128]{2,0,1:T(4,128)S(1)} %pad_maximum_fusion.17), channel_id=1, replica_groups=mesh['lat'=2,'lon'=16] {'lon'}, dimensions={2}, use_global_device_ids=true | all-gather | bytes 69632 | tf_op jit(solution)/shard_map/all_gather | solution.py:36
  202.2 2.3 copy.311
  204.6 2.3 gather_fusion.2
  207.6 11.5 %collective-permute-done.8 = f32[4,256,1]{2,1,0:T(8,128)S(1)} collective-permute-done((f32[4,256,1]{2,1,0:T(8,128)}, f32[4,256,1]{2,1,0:T(8,128)S(1)}, u32[]{:S(2)}, u32[]{:S(2)}) %collective-permute-start.8) | collective-permute-done | bytes 4128 | tf_op jit(solution)/shard_map/ppermute | solution.py:20
  219.1 2.2 collective-permute-done.9
  224.2 4.0 %collective-permute-start.15 = (f32[4,1,128]{2,1,0:T(1,128)S(1)}, f32[4,1,128]{2,1,0:T(1,128)S(1)}, u32[]{:S(2)}, u32[]{:S(2)}) collective-permute-start(f32[4,1,128]{2,1,0:T(1,128)S(1)} %get-tuple-element.23), channel_id=1, source_target_pairs={{16,0},{17,1},{18,2},{19,3},{20,4},{21,5},{22,6},{23,7},{24,8},{25... | collective-permute-start | bytes 6152 | tf_op jit(solution)/shard_map/ppermute | solution.py:22
  228.2 18.2 %all_gather.22 = f32[4,2,2048]{2,0,1:T(4,128)S(1)} all-gather(f32[4,2,128]{2,0,1:T(4,128)S(1)} %pad_maximum_fusion.18), channel_id=1, replica_groups=mesh['lat'=2,'lon'=16] {'lon'}, dimensions={2}, use_global_device_ids=true | all-gather | bytes 69632 | tf_op jit(solution)/shard_map/all_gather | solution.py:36
  246.4 2.3 copy.315
  248.8 2.3 gather_fusion.3
  251.7 11.5 %collective-permute-done.12 = f32[4,256,1]{2,1,0:T(8,128)S(1)} collective-permute-done((f32[4,256,1]{2,1,0:T(8,128)}, f32[4,256,1]{2,1,0:T(8,128)S(1)}, u32[]{:S(2)}, u32[]{:S(2)}) %collective-permute-start.12) | collective-permute-done | bytes 4128 | tf_op jit(solution)/shard_map/ppermute | solution.py:20
  263.3 2.2 collective-permute-done.13
  268.4 4.0 %collective-permute-start.19 = (f32[4,1,128]{2,1,0:T(1,128)S(1)}, f32[4,1,128]{2,1,0:T(1,128)S(1)}, u32[]{:S(2)}, u32[]{:S(2)}) collective-permute-start(f32[4,1,128]{2,1,0:T(1,128)S(1)} %get-tuple-element.17), channel_id=1, source_target_pairs={{16,0},{17,1},{18,2},{19,3},{20,4},{21,5},{22,6},{23,7},{24,8},{25... | collective-permute-start | bytes 6152 | tf_op jit(solution)/shard_map/ppermute | solution.py:22
  272.4 18.2 %all_gather.23 = f32[4,2,2048]{2,0,1:T(4,128)S(1)} all-gather(f32[4,2,128]{2,0,1:T(4,128)S(1)} %pad_maximum_fusion.19), channel_id=1, replica_groups=mesh['lat'=2,'lon'=16] {'lon'}, dimensions={2}, use_global_device_ids=true | all-gather | bytes 69632 | tf_op jit(solution)/shard_map/all_gather | solution.py:36
  290.6 2.3 copy.319
  292.9 2.3 gather_fusion.4
  295.9 11.5 %collective-permute-done.16 = f32[4,256,1]{2,1,0:T(8,128)S(1)} collective-permute-done((f32[4,256,1]{2,1,0:T(8,128)}, f32[4,256,1]{2,1,0:T(8,128)S(1)}, u32[]{:S(2)}, u32[]{:S(2)}) %collective-permute-start.16) | collective-permute-done | bytes 4128 | tf_op jit(solution)/shard_map/ppermute | solution.py:20
  307.5 2.2 collective-permute-done.17
  (94 shorter events, 26.9 us)
Async XLA Ops:
  7.2 8.7 %copy-start = (f32[4,256,128]{2,1,0:T(8,128)S(1)}, f32[4,256,128]{2,1,0:T(8,128)}, u32[]{:S(2)}) copy-start(f32[4,256,128]{2,1,0:T(8,128)} %param.8) | copy-start | bytes 1572868
  7.2 80.7 %all-gather.2.cloned.1.call-start = ((), (), s32[]{:S(2)}) async-start(), calls=%async_computation | async-start | bytes 2228224 | tf_op jit(solution)/shard_map/all_gather | solution.py:107
  8.0 35.2 %collective-permute-start.2 = (f32[4,1,128]{2,1,0:T(1,128)S(1)}, f32[4,1,128]{2,1,0:T(1,128)S(1)}, u32[]{:S(2)}, u32[]{:S(2)}) collective-permute-start(f32[4,1,128]{2,1,0:T(1,128)S(1)} %get-tuple-element.40), channel_id=1, source_target_pairs={{16,0},{17,1},{18,2},{19,3},{20,4},{21,5},{22,6},{23,7},{24,8},{25... | collective-permute-start | bytes 6152 | tf_op jit(solution)/shard_map/ppermute | solution.py:22
  9.3 33.9 %collective-permute-start.3 = (f32[4,1,128]{2,1,0:T(1,128)S(1)}, f32[4,1,128]{2,1,0:T(1,128)S(1)}, u32[]{:S(2)}, u32[]{:S(2)}) collective-permute-start(f32[4,1,128]{2,1,0:T(1,128)S(1)} %get-tuple-element.39), channel_id=1, source_target_pairs={{0,16},{1,17},{2,18},{3,19},{4,20},{5,21},{6,22},{7,23},{8,24},{9,... | collective-permute-start | bytes 6152 | tf_op jit(solution)/shard_map/ppermute | solution.py:20
  13.0 30.3 %collective-permute-start = (f32[4,256,1]{2,1,0:T(8,128)}, f32[4,256,1]{2,1,0:T(8,128)S(1)}, u32[]{:S(2)}, u32[]{:S(2)}) collective-permute-start(f32[4,256,1]{2,1,0:T(8,128)} %get-tuple-element.41), channel_id=1, source_target_pairs={{1,0},{2,1},{3,2},{4,3},{5,4},{6,5},{7,6},{8,7},{9,8},{10,9},{11,1... | collective-permute-start | bytes 12296 | tf_op jit(solution)/shard_map/ppermute | solution.py:22
  13.6 29.7 %collective-permute-start.1 = (f32[4,256,1]{2,1,0:T(8,128)}, f32[4,256,1]{2,1,0:T(8,128)}, u32[]{:S(2)}, u32[]{:S(2)}) collective-permute-start(f32[4,256,1]{2,1,0:T(8,128)} %get-tuple-element.42), channel_id=1, source_target_pairs={{0,1},{1,2},{2,3},{3,4},{4,5},{5,6},{6,7},{7,8},{8,9},{9,10},{10,1... | collective-permute-start | bytes 12296 | tf_op jit(solution)/shard_map/ppermute | solution.py:20
  43.3 0.8 copy-start.3
  44.1 3.0 copy-start.4
  87.8 22.8 %copy-start.5 = (f32[256,2048]{1,0:T(8,128)S(1)}, f32[256,2048]{1,0:T(8,128)}, u32[]{:S(2)}) copy-start(f32[256,2048]{1,0:T(8,128)} %all-gather.2.cloned.1.call-done) | copy-start | bytes 6291460
  132.0 7.5 %copy-start.1 = (f32[4,256,128]{2,1,0:T(8,128)}, f32[4,256,128]{2,1,0:T(8,128)S(1)}, u32[]{:S(2)}) copy-start(f32[4,256,128]{2,1,0:T(8,128)S(1)} %pad_maximum_fusion.14) | copy-start | bytes 1572868
  133.2 43.0 %copy-start.2 = (f32[4,256,128]{2,1,0:T(8,128)S(1)}, f32[4,256,128]{2,1,0:T(8,128)}, u32[]{:S(2)}) copy-start(f32[4,256,128]{2,1,0:T(8,128)} %param.11) | copy-start | bytes 1572868
  134.3 27.9 %collective-permute-start.6 = (f32[4,1,128]{2,1,0:T(1,128)S(1)}, f32[4,1,128]{2,1,0:T(1,128)S(1)}, u32[]{:S(2)}, u32[]{:S(2)}) collective-permute-start(f32[4,1,128]{2,1,0:T(1,128)S(1)} %slice.260), channel_id=1, source_target_pairs={{0,16},{1,17},{2,18},{3,19},{4,20},{5,21},{6,22},{7,23},{8,24},{9,... | collective-permute-start | bytes 6152 | tf_op jit(solution)/shard_map/ppermute | solution.py:20
  135.6 26.6 %collective-permute-start.7 = (f32[4,1,128]{2,1,0:T(1,128)S(1)}, f32[4,1,128]{2,1,0:T(1,128)S(1)}, u32[]{:S(2)}, u32[]{:S(2)}) collective-permute-start(f32[4,1,128]{2,1,0:T(1,128)S(1)} %slice.259), channel_id=1, source_target_pairs={{16,0},{17,1},{18,2},{19,3},{20,4},{21,5},{22,6},{23,7},{24,8},{25... | collective-permute-start | bytes 6152 | tf_op jit(solution)/shard_map/ppermute | solution.py:22
  161.6 12.1 %collective-permute-start.4 = (f32[4,256,1]{2,1,0:T(8,128)}, f32[4,256,1]{2,1,0:T(8,128)S(1)}, u32[]{:S(2)}, u32[]{:S(2)}) collective-permute-start(f32[4,256,1]{2,1,0:T(8,128)} %get-tuple-element.35), channel_id=1, source_target_pairs={{0,1},{1,2},{2,3},{3,4},{4,5},{5,6},{6,7},{7,8},{8,9},{9,10},{10,1... | collective-permute-start | bytes 12296 | tf_op jit(solution)/shard_map/ppermute | solution.py:20
  161.7 14.5 %collective-permute-start.5 = (f32[4,256,1]{2,1,0:T(8,128)}, f32[4,256,1]{2,1,0:T(8,128)S(1)}, u32[]{:S(2)}, u32[]{:S(2)}) collective-permute-start(f32[4,256,1]{2,1,0:T(8,128)} %get-tuple-element.36), channel_id=1, source_target_pairs={{1,0},{2,1},{3,2},{4,3},{5,4},{6,5},{7,6},{8,7},{9,8},{10,9},{11,1... | collective-permute-start | bytes 12296 | tf_op jit(solution)/shard_map/ppermute | solution.py:22
  179.0 28.6 %collective-permute-start.10 = (f32[4,1,128]{2,1,0:T(1,128)S(1)}, f32[4,1,128]{2,1,0:T(1,128)S(1)}, u32[]{:S(2)}, u32[]{:S(2)}) collective-permute-start(f32[4,1,128]{2,1,0:T(1,128)S(1)} %get-tuple-element.30), channel_id=1, source_target_pairs={{0,16},{1,17},{2,18},{3,19},{4,20},{5,21},{6,22},{7,23},{8,24},{9,... | collective-permute-start | bytes 6152 | tf_op jit(solution)/shard_map/ppermute | solution.py:20
  180.3 27.3 %collective-permute-start.11 = (f32[4,1,128]{2,1,0:T(1,128)S(1)}, f32[4,1,128]{2,1,0:T(1,128)S(1)}, u32[]{:S(2)}, u32[]{:S(2)}) collective-permute-start(f32[4,1,128]{2,1,0:T(1,128)S(1)} %get-tuple-element.29), channel_id=1, source_target_pairs={{16,0},{17,1},{18,2},{19,3},{20,4},{21,5},{22,6},{23,7},{24,8},{25... | collective-permute-start | bytes 6152 | tf_op jit(solution)/shard_map/ppermute | solution.py:22
  207.0 12.1 %collective-permute-start.8 = (f32[4,256,1]{2,1,0:T(8,128)}, f32[4,256,1]{2,1,0:T(8,128)S(1)}, u32[]{:S(2)}, u32[]{:S(2)}) collective-permute-start(f32[4,256,1]{2,1,0:T(8,128)} %get-tuple-element.31), channel_id=1, source_target_pairs={{0,1},{1,2},{2,3},{3,4},{4,5},{5,6},{6,7},{7,8},{8,9},{9,10},{10,1... | collective-permute-start | bytes 12296 | tf_op jit(solution)/shard_map/ppermute | solution.py:20
  207.1 14.3 %collective-permute-start.9 = (f32[4,256,1]{2,1,0:T(8,128)S(1)}, f32[4,256,1]{2,1,0:T(8,128)S(1)}, u32[]{:S(2)}, u32[]{:S(2)}) collective-permute-start(f32[4,256,1]{2,1,0:T(8,128)S(1)} %get-tuple-element.32), channel_id=1, source_target_pairs={{1,0},{2,1},{3,2},{4,3},{5,4},{6,5},{7,6},{8,7},{9,8},{10,9},{11,1... | collective-permute-start | bytes 12296 | tf_op jit(solution)/shard_map/ppermute | solution.py:22
  222.9 28.8 %collective-permute-start.14 = (f32[4,1,128]{2,1,0:T(1,128)S(1)}, f32[4,1,128]{2,1,0:T(1,128)S(1)}, u32[]{:S(2)}, u32[]{:S(2)}) collective-permute-start(f32[4,1,128]{2,1,0:T(1,128)S(1)} %get-tuple-element.24), channel_id=1, source_target_pairs={{0,16},{1,17},{2,18},{3,19},{4,20},{5,21},{6,22},{7,23},{8,24},{9,... | collective-permute-start | bytes 6152 | tf_op jit(solution)/shard_map/ppermute | solution.py:20
  224.2 27.5 %collective-permute-start.15 = (f32[4,1,128]{2,1,0:T(1,128)S(1)}, f32[4,1,128]{2,1,0:T(1,128)S(1)}, u32[]{:S(2)}, u32[]{:S(2)}) collective-permute-start(f32[4,1,128]{2,1,0:T(1,128)S(1)} %get-tuple-element.23), channel_id=1, source_target_pairs={{16,0},{17,1},{18,2},{19,3},{20,4},{21,5},{22,6},{23,7},{24,8},{25... | collective-permute-start | bytes 6152 | tf_op jit(solution)/shard_map/ppermute | solution.py:22
  251.2 12.1 %collective-permute-start.12 = (f32[4,256,1]{2,1,0:T(8,128)}, f32[4,256,1]{2,1,0:T(8,128)S(1)}, u32[]{:S(2)}, u32[]{:S(2)}) collective-permute-start(f32[4,256,1]{2,1,0:T(8,128)} %get-tuple-element.25), channel_id=1, source_target_pairs={{0,1},{1,2},{2,3},{3,4},{4,5},{5,6},{6,7},{7,8},{8,9},{9,10},{10,1... | collective-permute-start | bytes 12296 | tf_op jit(solution)/shard_map/ppermute | solution.py:20
  251.2 14.3 %collective-permute-start.13 = (f32[4,256,1]{2,1,0:T(8,128)S(1)}, f32[4,256,1]{2,1,0:T(8,128)S(1)}, u32[]{:S(2)}, u32[]{:S(2)}) collective-permute-start(f32[4,256,1]{2,1,0:T(8,128)S(1)} %get-tuple-element.26), channel_id=1, source_target_pairs={{1,0},{2,1},{3,2},{4,3},{5,4},{6,5},{7,6},{8,7},{9,8},{10,9},{11,1... | collective-permute-start | bytes 12296 | tf_op jit(solution)/shard_map/ppermute | solution.py:22
  267.1 28.8 %collective-permute-start.18 = (f32[4,1,128]{2,1,0:T(1,128)S(1)}, f32[4,1,128]{2,1,0:T(1,128)S(1)}, u32[]{:S(2)}, u32[]{:S(2)}) collective-permute-start(f32[4,1,128]{2,1,0:T(1,128)S(1)} %get-tuple-element.18), channel_id=1, source_target_pairs={{0,16},{1,17},{2,18},{3,19},{4,20},{5,21},{6,22},{7,23},{8,24},{9,... | collective-permute-start | bytes 6152 | tf_op jit(solution)/shard_map/ppermute | solution.py:20
  268.4 27.5 %collective-permute-start.19 = (f32[4,1,128]{2,1,0:T(1,128)S(1)}, f32[4,1,128]{2,1,0:T(1,128)S(1)}, u32[]{:S(2)}, u32[]{:S(2)}) collective-permute-start(f32[4,1,128]{2,1,0:T(1,128)S(1)} %get-tuple-element.17), channel_id=1, source_target_pairs={{16,0},{17,1},{18,2},{19,3},{20,4},{21,5},{22,6},{23,7},{24,8},{25... | collective-permute-start | bytes 6152 | tf_op jit(solution)/shard_map/ppermute | solution.py:22
  295.4 12.1 %collective-permute-start.16 = (f32[4,256,1]{2,1,0:T(8,128)}, f32[4,256,1]{2,1,0:T(8,128)S(1)}, u32[]{:S(2)}, u32[]{:S(2)}) collective-permute-start(f32[4,256,1]{2,1,0:T(8,128)} %get-tuple-element.19), channel_id=1, source_target_pairs={{0,1},{1,2},{2,3},{3,4},{4,5},{5,6},{6,7},{7,8},{8,9},{9,10},{10,1... | collective-permute-start | bytes 12296 | tf_op jit(solution)/shard_map/ppermute | solution.py:20
  295.4 14.3 %collective-permute-start.17 = (f32[4,256,1]{2,1,0:T(8,128)S(1)}, f32[4,256,1]{2,1,0:T(8,128)S(1)}, u32[]{:S(2)}, u32[]{:S(2)}) collective-permute-start(f32[4,256,1]{2,1,0:T(8,128)S(1)} %get-tuple-element.20), channel_id=1, source_target_pairs={{1,0},{2,1},{3,2},{4,3},{5,4},{6,5},{7,6},{8,7},{9,8},{10,9},{11,1... | collective-permute-start | bytes 12296 | tf_op jit(solution)/shard_map/ppermute | solution.py:22
Sparse Core Ops, SparseCore 0:
  47.2 40.5 all-gather.1
where the time goes:
time: 318 us
  blocking collectives  98.1 us (31%)
  waiting for transfers between devices  95.9 us (30%)
  matrix products  44 us (14%)
  starting transfers between devices  28.8 us (9%)
  local copies, waits for them, and re-layouts  28.6 us (9%)
  between operations  14.5 us (5%)
  other arithmetic  8 us (3%)
    all_gather x5, blocking collectives, neighbours(): whole_rows = lax.all_gather(edge_rows, 'lon', axis=2, tiled=True)  98.1 us
    ppermute x10, waiting for transfers between devices, padded(): lax.ppermute(tail, axis, [(i, (i + 1) % count) for i in range(ends)])  46.2 us
    all_gather x1, waiting for transfers between devices, polar_filter(): lax.all_gather(flat, 'lon', axis=1, tiled=True)  40.6 us
    dot_general x1, matrix products, project(): jnp.dot(rows, cosine, precision=lax.Precision.HIGHEST, preferred_element_...  21.2 us
    ppermute x10, starting transfers between devices, padded(): lax.ppermute(head, axis, [((i + 1) % count, i) for i in range(ends)])  19.9 us
    dot_general x1, matrix products, project(): jnp.dot(rows, sine, precision=lax.Precision.HIGHEST, preferred_element_ty...  19.7 us
    all_gather x5, local copies, waits for them, and re-layouts, neighbours(): whole_rows = lax.all_gather(edge_rows, 'lon', axis=2, tiled=True)  9.14 us
    ppermute x10, waiting for transfers between devices, padded(): lax.ppermute(head, axis, [((i + 1) % count, i) for i in range(ends)])  9.13 us
  transfers between devices with their start and end apart: 21, of which 9 were waited for; matrix products, arithmetic and copies ran while one was open for 7% of the time, Pallas kernels for 0%

commit v1 on v0

--- a/solution.py
+++ b/solution.py
@@ -33,7 +33,12 @@
     lat_padded = padded(field, (("lat", 1),), 1, False)
     edge_rows = jnp.stack([field[:, 0, :], field[:, -1, :]], axis=1)
     own_partner = lax.dynamic_slice_in_dim(partner, lon_index * width, width)
-    whole_rows = lax.all_gather(edge_rows, "lon", axis=2, tiled=True)
+    ring = [edge_rows]
+    for hop in range(15):
+        ring.append(lax.ppermute(ring[-1], "lon", [(dev, (dev + 1) % 16) for dev in range(16)]))
+    whole_rows = jnp.roll(
+        jnp.concatenate(ring[::-1], axis=2), (lax.axis_index("lon") + 1) * ring[0].shape[2], axis=2
+    )
     across = jnp.take(whole_rows, own_partner, axis=2)
     lat_index = lax.axis_index("lat")
     last_band = lax.axis_size("lat") - 1

time: 318 us -> 580 us (1.82); the launches traced: 318 us -> 572 us
  waiting for transfers between devices: 95.9 us -> 407 us
  blocking collectives: 98.1 us -> 0 us
  starting transfers between devices: 28.8 us -> 62.5 us
    ppermute x0 -> x75, waiting for transfers between devices: none -> 362 us  [neighbours(): lax.ppermute(ring[-1], 'lon', [(dev, (dev + 1) % 16) for dev in range(16)])]
    all_gather x5 -> x0, blocking collectives: 98.1 us -> none  [neighbours(): whole_rows = lax.all_gather(edge_rows, 'lon', axis=2, tiled=True)]
    ppermute x10, waiting for transfers between devices: 46.2 us -> 0.04 us  [padded(): lax.ppermute(tail, axis, [(i, (i + 1) % count) for i in range(ends)])]
    ppermute x10, starting transfers between devices: 19.9 us -> 43.5 us  [padded(): lax.ppermute(head, axis, [((i + 1) % count, i) for i in range(ends)])]
    ppermute x0 -> x75, starting transfers between devices: none -> 12.3 us  [neighbours(): lax.ppermute(ring[-1], 'lon', [(dev, (dev + 1) % 16) for dev in range(16)])]
    unnamed x12 -> x96, local copies, waits for them, and re-layouts: 0.8 us -> 12.2 us
    all_gather x5 -> x0, local copies, waits for them, and re-layouts: 9.14 us -> none  [neighbours(): whole_rows = lax.all_gather(edge_rows, 'lon', axis=2, tiled=True)]
    ppermute x10, waiting for transfers between devices: 9.13 us -> 1.76 us  [padded(): lax.ppermute(head, axis, [((i + 1) % count, i) for i in range(ends)])]
  transfers between devices with their start and end apart: 21 -> 96, of which waited for: 9 -> 75; matrix products, arithmetic and copies ran while one was open for 7% -> 5% of each run, Pallas kernels for 0% -> 0%
where the time goes in v1:
time: 580 us; the launch traced here: 572 us
  waiting for transfers between devices  407 us (70%)
  starting transfers between devices  62.5 us (11%)
  matrix products  44 us (8%)
  local copies, waits for them, and re-layouts  31.1 us (5%)
  between operations  15.3 us (3%)
  other arithmetic  12 us (2%)
    ppermute x75, waiting for transfers between devices, neighbours(): lax.ppermute(ring[-1], 'lon', [(dev, (dev + 1) % 16) for dev in range(16)])  362 us
    ppermute x10, starting transfers between devices, padded(): lax.ppermute(head, axis, [((i + 1) % count, i) for i in range(ends)])  43.5 us
    all_gather x1, waiting for transfers between devices, polar_filter(): lax.all_gather(flat, 'lon', axis=1, tiled=True)  43.3 us
    dot_general x1, matrix products, project(): jnp.dot(rows, cosine, precision=lax.Precision.HIGHEST, preferred_element_...  21.2 us
    dot_general x1, matrix products, project(): jnp.dot(rows, sine, precision=lax.Precision.HIGHEST, preferred_element_ty...  19.7 us
    ppermute x75, starting transfers between devices, neighbours(): lax.ppermute(ring[-1], 'lon', [(dev, (dev + 1) % 16) for dev in range(16)])  12.3 us
    unnamed x96, local copies, waits for them, and re-layouts  12.2 us
  transfers between devices with their start and end apart: 96, of which 75 were waited for; matrix products, arithmetic and copies ran while one was open for 5% of the time, Pallas kernels for 0%

profile of v1, /device:TPU:3, one launch (start us, length us, event | category | flops | bytes accessed | tf_op | source)
XLA Modules:
  0.0 571.6 jit_solution(9593816063227980935)
XLA Ops:
  20.9 5.7 %collective-permute-done.5 = f32[4,2,128]{2,0,1:T(4,128)S(1)} collective-permute-done((f32[4,2,128]{2,0,1:T(4,128)S(1)}, f32[4,2,128]{2,0,1:T(4,128)S(1)}, u32[]{:S(2)}, u32[]{:S(2)}) %collective-permute-start.5) | collective-permute-done | bytes 4128 | tf_op jit(solution)/shard_map/ppermute | solution.py:38
  26.6 5.7 %collective-permute-done.6 = f32[4,2,128]{2,0,1:T(4,128)S(1)} collective-permute-done((f32[4,2,128]{2,0,1:T(4,128)S(1)}, f32[4,2,128]{2,0,1:T(4,128)S(1)}, u32[]{:S(2)}, u32[]{:S(2)}) %collective-permute-start.6) | collective-permute-done | bytes 4128 | tf_op jit(solution)/shard_map/ppermute | solution.py:38
  32.3 5.7 %collective-permute-done.7 = f32[4,2,128]{2,0,1:T(4,128)S(1)} collective-permute-done((f32[4,2,128]{2,0,1:T(4,128)S(1)}, f32[4,2,128]{2,0,1:T(4,128)S(1)}, u32[]{:S(2)}, u32[]{:S(2)}) %collective-permute-start.7) | collective-permute-done | bytes 4128 | tf_op jit(solution)/shard_map/ppermute | solution.py:38
  38.1 5.7 %collective-permute-done.8 = f32[4,2,128]{2,0,1:T(4,128)S(1)} collective-permute-done((f32[4,2,128]{2,0,1:T(4,128)S(1)}, f32[4,2,128]{2,0,1:T(4,128)S(1)}, u32[]{:S(2)}, u32[]{:S(2)}) %collective-permute-start.8) | collective-permute-done | bytes 4128 | tf_op jit(solution)/shard_map/ppermute | solution.py:38
  43.8 5.7 %collective-permute-done.9 = f32[4,2,128]{2,0,1:T(4,128)S(1)} collective-permute-done((f32[4,2,128]{2,0,1:T(4,128)S(1)}, f32[4,2,128]{2,0,1:T(4,128)S(1)}, u32[]{:S(2)}, u32[]{:S(2)}) %collective-permute-start.9) | collective-permute-done | bytes 4128 | tf_op jit(solution)/shard_map/ppermute | solution.py:38
  49.5 5.7 %collective-permute-done.10 = f32[4,2,128]{2,0,1:T(4,128)S(1)} collective-permute-done((f32[4,2,128]{2,0,1:T(4,128)S(1)}, f32[4,2,128]{2,0,1:T(4,128)S(1)}, u32[]{:S(2)}, u32[]{:S(2)}) %collective-permute-start.10) | collective-permute-done | bytes 4128 | tf_op jit(solution)/shard_map/ppermute | solution.py:38
  55.2 5.7 %collective-permute-done.11 = f32[4,2,128]{2,0,1:T(4,128)S(1)} collective-permute-done((f32[4,2,128]{2,0,1:T(4,128)S(1)}, f32[4,2,128]{2,0,1:T(4,128)S(1)}, u32[]{:S(2)}, u32[]{:S(2)}) %collective-permute-start.11) | collective-permute-done | bytes 4128 | tf_op jit(solution)/shard_map/ppermute | solution.py:38
  83.8 7.0 %collective-permute-done.15 = f32[4,2,128]{2,0,1:T(4,128)S(1)} collective-permute-done((f32[4,2,128]{2,0,1:T(4,128)S(1)}, f32[4,2,128]{2,0,1:T(4,128)S(1)}, u32[]{:S(2)}, u32[]{:S(2)}) %collective-permute-start.15) | collective-permute-done | bytes 4128 | tf_op jit(solution)/shard_map/ppermute | solution.py:38
  103.3 43.3 %all-gather.2.cloned.1.call-done = f32[256,2048]{1,0:T(8,128)} async-done(((f32[256,128]{1,0:T(8,128)}), f32[256,2048]{1,0:T(8,128)}) %all-gather.2.cloned.1.call-update) | async-done | bytes 2097168 | tf_op jit(solution)/shard_map/all_gather | solution.py:112
  146.6 21.2 %fusion.12 = f32[256,512]{1,0:T(8,128)S(1)} fusion(f32[256,2048]{1,0:T(8,128)} %all-gather.2.cloned.1.call-done, f32[512]{0:T(512)S(1)} %select_multiply_fusion, s32[256]{0:T(256)S(1)} %le.23), kind=kOutput, calls=%fused_computation.18 | convolution fusion | flops 3236298752 | bytes 2624512 | tf_op jit(solution)/shard_map/dot_general | solution.py:64
  169.4 19.7 %fusion.15 = f32[256,512]{1,0:T(8,128)S(1)} fusion(f32[256,2048]{1,0:T(8,128)S(1)} %copy-done.7, f32[512]{0:T(512)S(1)} %select_multiply_fusion, s32[256]{0:T(256)S(1)} %le.23), kind=kOutput, calls=%fused_computation.19 | convolution fusion | flops 3236298752 | bytes 2624512 | tf_op jit(solution)/shard_map/dot_general | solution.py:67
  203.1 5.7 %collective-permute-done.24 = f32[4,2,128]{2,0,1:T(4,128)S(1)} collective-permute-done((f32[4,2,128]{2,0,1:T(4,128)S(1)}, f32[4,2,128]{2,0,1:T(4,128)S(1)}, u32[]{:S(2)}, u32[]{:S(2)}) %collective-permute-start.24) | collective-permute-done | bytes 4128 | tf_op jit(solution)/shard_map/ppermute | solution.py:38
  208.9 5.7 %collective-permute-done.25 = f32[4,2,128]{2,0,1:T(4,128)S(1)} collective-permute-done((f32[4,2,128]{2,0,1:T(4,128)S(1)}, f32[4,2,128]{2,0,1:T(4,128)S(1)}, u32[]{:S(2)}, u32[]{:S(2)}) %collective-permute-start.25) | collective-permute-done | bytes 4128 | tf_op jit(solution)/shard_map/ppermute | solution.py:38
  214.6 5.7 %collective-permute-done.26 = f32[4,2,128]{2,0,1:T(4,128)S(1)} collective-permute-done((f32[4,2,128]{2,0,1:T(4,128)S(1)}, f32[4,2,128]{2,0,1:T(4,128)S(1)}, u32[]{:S(2)}, u32[]{:S(2)}) %collective-permute-start.26) | collective-permute-done | bytes 4128 | tf_op jit(solution)/shard_map/ppermute | solution.py:38
  220.3 5.7 %collective-permute-done.27 = f32[4,2,128]{2,0,1:T(4,128)S(1)} collective-permute-done((f32[4,2,128]{2,0,1:T(4,128)S(1)}, f32[4,2,128]{2,0,1:T(4,128)S(1)}, u32[]{:S(2)}, u32[]{:S(2)}) %collective-permute-start.27) | collective-permute-done | bytes 4128 | tf_op jit(solution)/shard_map/ppermute | solution.py:38
  226.1 5.7 %collective-permute-done.28 = f32[4,2,128]{2,0,1:T(4,128)S(1)} collective-permute-done((f32[4,2,128]{2,0,1:T(4,128)S(1)}, f32[4,2,128]{2,0,1:T(4,128)S(1)}, u32[]{:S(2)}, u32[]{:S(2)}) %collective-permute-start.28) | collective-permute-done | bytes 4128 | tf_op jit(solution)/shard_map/ppermute | solution.py:38
  231.8 5.7 %collective-permute-done.29 = f32[4,2,128]{2,0,1:T(4,128)S(1)} collective-permute-done((f32[4,2,128]{2,0,1:T(4,128)S(1)}, f32[4,2,128]{2,0,1:T(4,128)S(1)}, u32[]{:S(2)}, u32[]{:S(2)}) %collective-permute-start.29) | collective-permute-done | bytes 4128 | tf_op jit(solution)/shard_map/ppermute | solution.py:38
  237.5 5.7 %collective-permute-done.30 = f32[4,2,128]{2,0,1:T(4,128)S(1)} collective-permute-done((f32[4,2,128]{2,0,1:T(4,128)S(1)}, f32[4,2,128]{2,0,1:T(4,128)S(1)}, u32[]{:S(2)}, u32[]{:S(2)}) %collective-permute-start.30) | collective-permute-done | bytes 4128 | tf_op jit(solution)/shard_map/ppermute | solution.py:38
  243.3 5.7 %collective-permute-done.31 = f32[4,2,128]{2,0,1:T(4,128)S(1)} collective-permute-done((f32[4,2,128]{2,0,1:T(4,128)S(1)}, f32[4,2,128]{2,0,1:T(4,128)S(1)}, u32[]{:S(2)}, u32[]{:S(2)}) %collective-permute-start.31) | collective-permute-done | bytes 4128 | tf_op jit(solution)/shard_map/ppermute | solution.py:38
  254.8 5.9 %collective-permute-done.33 = f32[4,2,128]{2,0,1:T(4,128)S(1)} collective-permute-done((f32[4,2,128]{2,0,1:T(4,128)S(1)}, f32[4,2,128]{2,0,1:T(4,128)S(1)}, u32[]{:S(2)}, u32[]{:S(2)}) %collective-permute-start.33) | collective-permute-done | bytes 4128 | tf_op jit(solution)/shard_map/ppermute | solution.py:38
  278.7 8.3 %collective-permute-done.40 = f32[4,2,128]{2,0,1:T(4,128)S(1)} collective-permute-done((f32[4,2,128]{2,0,1:T(4,128)S(1)}, f32[4,2,128]{2,0,1:T(4,128)S(1)}, u32[]{:S(2)}, u32[]{:S(2)}) %collective-permute-start.40) | collective-permute-done | bytes 4128 | tf_op jit(solution)/shard_map/ppermute | solution.py:38
  375.1 6.6 %collective-permute-done.59 = f32[4,2,128]{2,0,1:T(4,128)S(1)} collective-permute-done((f32[4,2,128]{2,0,1:T(4,128)S(1)}, f32[4,2,128]{2,0,1:T(4,128)S(1)}, u32[]{:S(2)}, u32[]{:S(2)}) %collective-permute-start.59) | collective-permute-done | bytes 4128 | tf_op jit(solution)/shard_map/ppermute | solution.py:38
  387.4 5.7 %collective-permute-done.61 = f32[4,2,128]{2,0,1:T(4,128)S(1)} collective-permute-done((f32[4,2,128]{2,0,1:T(4,128)S(1)}, f32[4,2,128]{2,0,1:T(4,128)S(1)}, u32[]{:S(2)}, u32[]{:S(2)}) %collective-permute-start.61) | collective-permute-done | bytes 4128 | tf_op jit(solution)/shard_map/ppermute | solution.py:38
  393.1 5.7 %collective-permute-done.62 = f32[4,2,128]{2,0,1:T(4,128)S(1)} collective-permute-done((f32[4,2,128]{2,0,1:T(4,128)S(1)}, f32[4,2,128]{2,0,1:T(4,128)S(1)}, u32[]{:S(2)}, u32[]{:S(2)}) %collective-permute-start.62) | collective-permute-done | bytes 4128 | tf_op jit(solution)/shard_map/ppermute | solution.py:38
  398.8 5.7 %collective-permute-done.63 = f32[4,2,128]{2,0,1:T(4,128)S(1)} collective-permute-done((f32[4,2,128]{2,0,1:T(4,128)S(1)}, f32[4,2,128]{2,0,1:T(4,128)S(1)}, u32[]{:S(2)}, u32[]{:S(2)}) %collective-permute-start.63) | collective-permute-done | bytes 4128 | tf_op jit(solution)/shard_map/ppermute | solution.py:38
  404.6 5.7 %collective-permute-done.64 = f32[4,2,128]{2,0,1:T(4,128)S(1)} collective-permute-done((f32[4,2,128]{2,0,1:T(4,128)S(1)}, f32[4,2,128]{2,0,1:T(4,128)S(1)}, u32[]{:S(2)}, u32[]{:S(2)}) %collective-permute-start.64) | collective-permute-done | bytes 4128 | tf_op jit(solution)/shard_map/ppermute | solution.py:38
  410.3 5.7 %collective-permute-done.65 = f32[4,2,128]{2,0,1:T(4,128)S(1)} collective-permute-done((f32[4,2,128]{2,0,1:T(4,128)S(1)}, f32[4,2,128]{2,0,1:T(4,128)S(1)}, u32[]{:S(2)}, u32[]{:S(2)}) %collective-permute-start.65) | collective-permute-done | bytes 4128 | tf_op jit(solution)/shard_map/ppermute | solution.py:38
  416.0 5.7 %collective-permute-done.66 = f32[4,2,128]{2,0,1:T(4,128)S(1)} collective-permute-done((f32[4,2,128]{2,0,1:T(4,128)S(1)}, f32[4,2,128]{2,0,1:T(4,128)S(1)}, u32[]{:S(2)}, u32[]{:S(2)}) %collective-permute-start.66) | collective-permute-done | bytes 4128 | tf_op jit(solution)/shard_map/ppermute | solution.py:38
  421.8 5.7 %collective-permute-done.67 = f32[4,2,128]{2,0,1:T(4,128)S(1)} collective-permute-done((f32[4,2,128]{2,0,1:T(4,128)S(1)}, f32[4,2,128]{2,0,1:T(4,128)S(1)}, u32[]{:S(2)}, u32[]{:S(2)}) %collective-permute-start.67) | collective-permute-done | bytes 4128 | tf_op jit(solution)/shard_map/ppermute | solution.py:38
  427.5 5.7 %collective-permute-done.68 = f32[4,2,128]{2,0,1:T(4,128)S(1)} collective-permute-done((f32[4,2,128]{2,0,1:T(4,128)S(1)}, f32[4,2,128]{2,0,1:T(4,128)S(1)}, u32[]{:S(2)}, u32[]{:S(2)}) %collective-permute-start.68) | collective-permute-done | bytes 4128 | tf_op jit(solution)/shard_map/ppermute | solution.py:38
  433.2 5.7 %collective-permute-done.69 = f32[4,2,128]{2,0,1:T(4,128)S(1)} collective-permute-done((f32[4,2,128]{2,0,1:T(4,128)S(1)}, f32[4,2,128]{2,0,1:T(4,128)S(1)}, u32[]{:S(2)}, u32[]{:S(2)}) %collective-permute-start.69) | collective-permute-done | bytes 4128 | tf_op jit(solution)/shard_map/ppermute | solution.py:38
  469.8 6.6 %collective-permute-done.78 = f32[4,2,128]{2,0,1:T(4,128)S(1)} collective-permute-done((f32[4,2,128]{2,0,1:T(4,128)S(1)}, f32[4,2,128]{2,0,1:T(4,128)S(1)}, u32[]{:S(2)}, u32[]{:S(2)}) %collective-permute-start.78) | collective-permute-done | bytes 4128 | tf_op jit(solution)/shard_map/ppermute | solution.py:38
  (328 shorter events, 300.5 us)
Async XLA Ops:
  7.2 139.4 %all-gather.2.cloned.1.call-start = ((), (), s32[]{:S(2)}) async-start(), calls=%async_computation | async-start | bytes 2228224 | tf_op jit(solution)/shard_map/all_gather | solution.py:112
  61.0 38.3 %collective-permute-start.17 = (f32[4,1,128]{2,1,0:T(1,128)S(1)}, f32[4,1,128]{2,1,0:T(1,128)S(1)}, u32[]{:S(2)}, u32[]{:S(2)}) collective-permute-start(f32[4,1,128]{2,1,0:T(1,128)S(1)} %get-tuple-element.41), channel_id=1, source_target_pairs={{16,0},{17,1},{18,2},{19,3},{20,4},{21,5},{22,6},{23,7},{24,8},{25... | collective-permute-start | bytes 6152 | tf_op jit(solution)/shard_map/ppermute | solution.py:22
  62.7 36.6 %collective-permute-start.18 = (f32[4,1,128]{2,1,0:T(1,128)S(1)}, f32[4,1,128]{2,1,0:T(1,128)S(1)}, u32[]{:S(2)}, u32[]{:S(2)}) collective-permute-start(f32[4,1,128]{2,1,0:T(1,128)S(1)} %get-tuple-element.40), channel_id=1, source_target_pairs={{0,16},{1,17},{2,18},{3,19},{4,20},{5,21},{6,22},{7,23},{8,24},{9,... | collective-permute-start | bytes 6152 | tf_op jit(solution)/shard_map/ppermute | solution.py:20
  66.7 7.4 %collective-permute-start.13 = (f32[4,2,128]{2,0,1:T(4,128)S(1)}, f32[4,2,128]{2,0,1:T(4,128)S(1)}, u32[]{:S(2)}, u32[]{:S(2)}) collective-permute-start(f32[4,2,128]{2,0,1:T(4,128)S(1)} %collective-permute-done.12), channel_id=1, source_target_pairs={{0,1},{1,2},{2,3},{3,4},{4,5},{5,6},{6,7},{7,8},{8,9},{9,10},{10,1... | collective-permute-start | bytes 12296 | tf_op jit(solution)/shard_map/ppermute | solution.py:38
  69.1 30.3 %collective-permute-start = (f32[4,256,1]{2,1,0:T(8,128)}, f32[4,256,1]{2,1,0:T(8,128)S(1)}, u32[]{:S(2)}, u32[]{:S(2)}) collective-permute-start(f32[4,256,1]{2,1,0:T(8,128)} %get-tuple-element.42), channel_id=1, source_target_pairs={{1,0},{2,1},{3,2},{4,3},{5,4},{6,5},{7,6},{8,7},{9,8},{10,9},{11,1... | collective-permute-start | bytes 12296 | tf_op jit(solution)/shard_map/ppermute | solution.py:22
  74.1 25.2 %collective-permute-start.1 = (f32[4,256,1]{2,1,0:T(8,128)}, f32[4,256,1]{2,1,0:T(8,128)}, u32[]{:S(2)}, u32[]{:S(2)}) collective-permute-start(f32[4,256,1]{2,1,0:T(8,128)} %get-tuple-element.43), channel_id=1, source_target_pairs={{0,1},{1,2},{2,3},{3,4},{4,5},{5,6},{6,7},{7,8},{8,9},{9,10},{10,1... | collective-permute-start | bytes 12296 | tf_op jit(solution)/shard_map/ppermute | solution.py:20
  74.1 6.4 %collective-permute-start.14 = (f32[4,2,128]{2,0,1:T(4,128)S(1)}, f32[4,2,128]{2,0,1:T(4,128)S(1)}, u32[]{:S(2)}, u32[]{:S(2)}) collective-permute-start(f32[4,2,128]{2,0,1:T(4,128)S(1)} %collective-permute-done.13), channel_id=1, source_target_pairs={{0,1},{1,2},{2,3},{3,4},{4,5},{5,6},{6,7},{7,8},{8,9},{9,10},{10,1... | collective-permute-start | bytes 12296 | tf_op jit(solution)/shard_map/ppermute | solution.py:38
  80.6 10.3 %collective-permute-start.15 = (f32[4,2,128]{2,0,1:T(4,128)S(1)}, f32[4,2,128]{2,0,1:T(4,128)S(1)}, u32[]{:S(2)}, u32[]{:S(2)}) collective-permute-start(f32[4,2,128]{2,0,1:T(4,128)S(1)} %collective-permute-done.14), channel_id=1, source_target_pairs={{0,1},{1,2},{2,3},{3,4},{4,5},{5,6},{6,7},{7,8},{8,9},{9,10},{10,1... | collective-permute-start | bytes 12296 | tf_op jit(solution)/shard_map/ppermute | solution.py:38
  90.8 6.2 %collective-permute-start.16 = (f32[4,2,128]{2,0,1:T(4,128)S(1)}, f32[4,2,128]{2,0,1:T(4,128)S(1)}, u32[]{:S(2)}, u32[]{:S(2)}) collective-permute-start(f32[4,2,128]{2,0,1:T(4,128)S(1)} %collective-permute-done.15), channel_id=1, source_target_pairs={{0,1},{1,2},{2,3},{3,4},{4,5},{5,6},{6,7},{7,8},{8,9},{9,10},{10,1... | collective-permute-start | bytes 12296 | tf_op jit(solution)/shard_map/ppermute | solution.py:38
  249.0 25.8 %collective-permute-start.36 = (f32[4,1,128]{2,1,0:T(1,128)S(1)}, f32[4,1,128]{2,1,0:T(1,128)S(1)}, u32[]{:S(2)}, u32[]{:S(2)}) collective-permute-start(f32[4,1,128]{2,1,0:T(1,128)S(1)} %slice.260), channel_id=1, source_target_pairs={{0,16},{1,17},{2,18},{3,19},{4,20},{5,21},{6,22},{7,23},{8,24},{9,... | collective-permute-start | bytes 6152 | tf_op jit(solution)/shard_map/ppermute | solution.py:20
  250.3 24.5 %collective-permute-start.37 = (f32[4,1,128]{2,1,0:T(1,128)S(1)}, f32[4,1,128]{2,1,0:T(1,128)S(1)}, u32[]{:S(2)}, u32[]{:S(2)}) collective-permute-start(f32[4,1,128]{2,1,0:T(1,128)S(1)} %slice.259), channel_id=1, source_target_pairs={{16,0},{17,1},{18,2},{19,3},{20,4},{21,5},{22,6},{23,7},{24,8},{25... | collective-permute-start | bytes 6152 | tf_op jit(solution)/shard_map/ppermute | solution.py:22
  254.7 5.9 %collective-permute-start.33 = (f32[4,2,128]{2,0,1:T(4,128)S(1)}, f32[4,2,128]{2,0,1:T(4,128)S(1)}, u32[]{:S(2)}, u32[]{:S(2)}) collective-permute-start(f32[4,2,128]{2,0,1:T(4,128)S(1)} %collective-permute-done.32), channel_id=1, source_target_pairs={{0,1},{1,2},{2,3},{3,4},{4,5},{5,6},{6,7},{7,8},{8,9},{9,10},{10,1... | collective-permute-start | bytes 12296 | tf_op jit(solution)/shard_map/ppermute | solution.py:38
  266.4 6.2 %collective-permute-start.35 = (f32[4,2,128]{2,0,1:T(4,128)S(1)}, f32[4,2,128]{2,0,1:T(4,128)S(1)}, u32[]{:S(2)}, u32[]{:S(2)}) collective-permute-start(f32[4,2,128]{2,0,1:T(4,128)S(1)} %collective-permute-done.34), channel_id=1, source_target_pairs={{0,1},{1,2},{2,3},{3,4},{4,5},{5,6},{6,7},{7,8},{8,9},{9,10},{10,1... | collective-permute-start | bytes 12296 | tf_op jit(solution)/shard_map/ppermute | solution.py:38
  267.4 7.4 %collective-permute-start.19 = (f32[4,256,1]{2,1,0:T(8,128)}, f32[4,256,1]{2,1,0:T(8,128)}, u32[]{:S(2)}, u32[]{:S(2)}) collective-permute-start(f32[4,256,1]{2,1,0:T(8,128)} %get-tuple-element.36), channel_id=1, source_target_pairs={{0,1},{1,2},{2,3},{3,4},{4,5},{5,6},{6,7},{7,8},{8,9},{9,10},{10,1... | collective-permute-start | bytes 12296 | tf_op jit(solution)/shard_map/ppermute | solution.py:20
  267.4 9.2 %collective-permute-start.20 = (f32[4,256,1]{2,1,0:T(8,128)}, f32[4,256,1]{2,1,0:T(8,128)}, u32[]{:S(2)}, u32[]{:S(2)}) collective-permute-start(f32[4,256,1]{2,1,0:T(8,128)} %get-tuple-element.37), channel_id=1, source_target_pairs={{1,0},{2,1},{3,2},{4,3},{5,4},{6,5},{7,6},{8,7},{9,8},{10,9},{11,1... | collective-permute-start | bytes 12296 | tf_op jit(solution)/shard_map/ppermute | solution.py:22
  278.6 8.4 %collective-permute-start.40 = (f32[4,2,128]{2,0,1:T(4,128)S(1)}, f32[4,2,128]{2,0,1:T(4,128)S(1)}, u32[]{:S(2)}, u32[]{:S(2)}) collective-permute-start(f32[4,2,128]{2,0,1:T(4,128)S(1)} %pad_maximum_fusion.17), channel_id=1, source_target_pairs={{0,1},{1,2},{2,3},{3,4},{4,5},{5,6},{6,7},{7,8},{8,9},{9,10},{10,1... | collective-permute-start | bytes 12296 | tf_op jit(solution)/shard_map/ppermute | solution.py:38
  350.0 22.5 %collective-permute-start.55 = (f32[4,1,128]{2,1,0:T(1,128)S(1)}, f32[4,1,128]{2,1,0:T(1,128)S(1)}, u32[]{:S(2)}, u32[]{:S(2)}) collective-permute-start(f32[4,1,128]{2,1,0:T(1,128)S(1)} %get-tuple-element.31), channel_id=1, source_target_pairs={{0,16},{1,17},{2,18},{3,19},{4,20},{5,21},{6,22},{7,23},{8,24},{9,... | collective-permute-start | bytes 6152 | tf_op jit(solution)/shard_map/ppermute | solution.py:20
  351.3 21.2 %collective-permute-start.56 = (f32[4,1,128]{2,1,0:T(1,128)S(1)}, f32[4,1,128]{2,1,0:T(1,128)S(1)}, u32[]{:S(2)}, u32[]{:S(2)}) collective-permute-start(f32[4,1,128]{2,1,0:T(1,128)S(1)} %get-tuple-element.30), channel_id=1, source_target_pairs={{16,0},{17,1},{18,2},{19,3},{20,4},{21,5},{22,6},{23,7},{24,8},{25... | collective-permute-start | bytes 6152 | tf_op jit(solution)/shard_map/ppermute | solution.py:22
  361.7 10.8 %collective-permute-start.38 = (f32[4,256,1]{2,1,0:T(8,128)}, f32[4,256,1]{2,1,0:T(8,128)S(1)}, u32[]{:S(2)}, u32[]{:S(2)}) collective-permute-start(f32[4,256,1]{2,1,0:T(8,128)} %get-tuple-element.32), channel_id=1, source_target_pairs={{0,1},{1,2},{2,3},{3,4},{4,5},{5,6},{6,7},{7,8},{8,9},{9,10},{10,1... | collective-permute-start | bytes 12296 | tf_op jit(solution)/shard_map/ppermute | solution.py:20
  361.8 10.8 %collective-permute-start.39 = (f32[4,256,1]{2,1,0:T(8,128)}, f32[4,256,1]{2,1,0:T(8,128)}, u32[]{:S(2)}, u32[]{:S(2)}) collective-permute-start(f32[4,256,1]{2,1,0:T(8,128)} %get-tuple-element.33), channel_id=1, source_target_pairs={{1,0},{2,1},{3,2},{4,3},{5,4},{6,5},{7,6},{8,7},{9,8},{10,9},{11,1... | collective-permute-start | bytes 12296 | tf_op jit(solution)/shard_map/ppermute | solution.py:22
  375.0 6.6 %collective-permute-start.59 = (f32[4,2,128]{2,0,1:T(4,128)S(1)}, f32[4,2,128]{2,0,1:T(4,128)S(1)}, u32[]{:S(2)}, u32[]{:S(2)}) collective-permute-start(f32[4,2,128]{2,0,1:T(4,128)S(1)} %pad_maximum_fusion.18), channel_id=1, source_target_pairs={{0,1},{1,2},{2,3},{3,4},{4,5},{5,6},{6,7},{7,8},{8,9},{9,10},{10,1... | collective-permute-start | bytes 12296 | tf_op jit(solution)/shard_map/ppermute | solution.py:38
  444.7 22.5 %collective-permute-start.74 = (f32[4,1,128]{2,1,0:T(1,128)S(1)}, f32[4,1,128]{2,1,0:T(1,128)S(1)}, u32[]{:S(2)}, u32[]{:S(2)}) collective-permute-start(f32[4,1,128]{2,1,0:T(1,128)S(1)} %get-tuple-element.25), channel_id=1, source_target_pairs={{0,16},{1,17},{2,18},{3,19},{4,20},{5,21},{6,22},{7,23},{8,24},{9,... | collective-permute-start | bytes 6152 | tf_op jit(solution)/shard_map/ppermute | solution.py:20
  446.0 21.2 %collective-permute-start.75 = (f32[4,1,128]{2,1,0:T(1,128)S(1)}, f32[4,1,128]{2,1,0:T(1,128)S(1)}, u32[]{:S(2)}, u32[]{:S(2)}) collective-permute-start(f32[4,1,128]{2,1,0:T(1,128)S(1)} %get-tuple-element.24), channel_id=1, source_target_pairs={{16,0},{17,1},{18,2},{19,3},{20,4},{21,5},{22,6},{23,7},{24,8},{25... | collective-permute-start | bytes 6152 | tf_op jit(solution)/shard_map/ppermute | solution.py:22
  456.4 10.8 %collective-permute-start.57 = (f32[4,256,1]{2,1,0:T(8,128)}, f32[4,256,1]{2,1,0:T(8,128)S(1)}, u32[]{:S(2)}, u32[]{:S(2)}) collective-permute-start(f32[4,256,1]{2,1,0:T(8,128)} %get-tuple-element.26), channel_id=1, source_target_pairs={{0,1},{1,2},{2,3},{3,4},{4,5},{5,6},{6,7},{7,8},{8,9},{9,10},{10,1... | collective-permute-start | bytes 12296 | tf_op jit(solution)/shard_map/ppermute | solution.py:20
  456.5 10.8 %collective-permute-start.58 = (f32[4,256,1]{2,1,0:T(8,128)}, f32[4,256,1]{2,1,0:T(8,128)}, u32[]{:S(2)}, u32[]{:S(2)}) collective-permute-start(f32[4,256,1]{2,1,0:T(8,128)} %get-tuple-element.27), channel_id=1, source_target_pairs={{1,0},{2,1},{3,2},{4,3},{5,4},{6,5},{7,6},{8,7},{9,8},{10,9},{11,1... | collective-permute-start | bytes 12296 | tf_op jit(solution)/shard_map/ppermute | solution.py:22
  469.7 6.6 %collective-permute-start.78 = (f32[4,2,128]{2,0,1:T(4,128)S(1)}, f32[4,2,128]{2,0,1:T(4,128)S(1)}, u32[]{:S(2)}, u32[]{:S(2)}) collective-permute-start(f32[4,2,128]{2,0,1:T(4,128)S(1)} %pad_maximum_fusion.19), channel_id=1, source_target_pairs={{0,1},{1,2},{2,3},{3,4},{4,5},{5,6},{6,7},{7,8},{8,9},{9,10},{10,1... | collective-permute-start | bytes 12296 | tf_op jit(solution)/shard_map/ppermute | solution.py:38
  510.7 6.0 %collective-permute-start.85 = (f32[4,2,128]{2,0,1:T(4,128)S(1)}, f32[4,2,128]{2,0,1:T(4,128)S(1)}, u32[]{:S(2)}, u32[]{:S(2)}) collective-permute-start(f32[4,2,128]{2,0,1:T(4,128)S(1)} %collective-permute-done.84), channel_id=1, source_target_pairs={{0,1},{1,2},{2,3},{3,4},{4,5},{5,6},{6,7},{7,8},{8,9},{9,10},{10,1... | collective-permute-start | bytes 12296 | tf_op jit(solution)/shard_map/ppermute | solution.py:38
  539.6 22.5 %collective-permute-start.93 = (f32[4,1,128]{2,1,0:T(1,128)S(1)}, f32[4,1,128]{2,1,0:T(1,128)S(1)}, u32[]{:S(2)}, u32[]{:S(2)}) collective-permute-start(f32[4,1,128]{2,1,0:T(1,128)S(1)} %get-tuple-element.19), channel_id=1, source_target_pairs={{0,16},{1,17},{2,18},{3,19},{4,20},{5,21},{6,22},{7,23},{8,24},{9,... | collective-permute-start | bytes 6152 | tf_op jit(solution)/shard_map/ppermute | solution.py:20
  540.9 21.2 %collective-permute-start.94 = (f32[4,1,128]{2,1,0:T(1,128)S(1)}, f32[4,1,128]{2,1,0:T(1,128)S(1)}, u32[]{:S(2)}, u32[]{:S(2)}) collective-permute-start(f32[4,1,128]{2,1,0:T(1,128)S(1)} %get-tuple-element.18), channel_id=1, source_target_pairs={{16,0},{17,1},{18,2},{19,3},{20,4},{21,5},{22,6},{23,7},{24,8},{25... | collective-permute-start | bytes 6152 | tf_op jit(solution)/shard_map/ppermute | solution.py:22
  545.3 5.9 %collective-permute-start.91 = (f32[4,2,128]{2,0,1:T(4,128)S(1)}, f32[4,2,128]{2,0,1:T(4,128)S(1)}, u32[]{:S(2)}, u32[]{:S(2)}) collective-permute-start(f32[4,2,128]{2,0,1:T(4,128)S(1)} %collective-permute-done.90), channel_id=1, source_target_pairs={{0,1},{1,2},{2,3},{3,4},{4,5},{5,6},{6,7},{7,8},{8,9},{9,10},{10,1... | collective-permute-start | bytes 12296 | tf_op jit(solution)/shard_map/ppermute | solution.py:38
  551.3 10.8 %collective-permute-start.76 = (f32[4,256,1]{2,1,0:T(8,128)}, f32[4,256,1]{2,1,0:T(8,128)S(1)}, u32[]{:S(2)}, u32[]{:S(2)}) collective-permute-start(f32[4,256,1]{2,1,0:T(8,128)} %get-tuple-element.20), channel_id=1, source_target_pairs={{0,1},{1,2},{2,3},{3,4},{4,5},{5,6},{6,7},{7,8},{8,9},{9,10},{10,1... | collective-permute-start | bytes 12296 | tf_op jit(solution)/shard_map/ppermute | solution.py:20
  551.4 10.8 %collective-permute-start.77 = (f32[4,256,1]{2,1,0:T(8,128)}, f32[4,256,1]{2,1,0:T(8,128)}, u32[]{:S(2)}, u32[]{:S(2)}) collective-permute-start(f32[4,256,1]{2,1,0:T(8,128)} %get-tuple-element.21), channel_id=1, source_target_pairs={{1,0},{2,1},{3,2},{4,3},{5,4},{6,5},{7,6},{8,7},{9,8},{10,9},{11,1... | collective-permute-start | bytes 12296 | tf_op jit(solution)/shard_map/ppermute | solution.py:22
  (72 other events, 480.9 us)
Sparse Core Ops, SparseCore 0:
  103.3 43.2 all-gather.1
